TPU v7x, 256 devices: a whole 4x4x8 slice. The times are simulated.
256 devices in a mesh: grp: 8 (over z), seq: 32 (over y, x, core).
Axes of the slice: x: 4, y: 4, z: 8, core: 2. Of those that a mesh axis runs over, the one named last changes fastest.
Arguments:
- queries: bfloat16 [64, 4, 64, 576], P('grp'), parts along dimension 0, may hold values from -190 to 190
- latent_cache: bfloat16 [64, 32768, 576], P('grp', 'seq'), parts along dimension 0, may hold values from -4 to 4
- context_lengths: int32 [64], P('grp'), parts along dimension 0, may hold values from 8192 to 32768, as said below
- value_up: bfloat16 [64, 512, 128], P('seq'), may hold values from -0.5 to 0.5
- output_projection_rows: bfloat16 [8192, 7168], P('seq'), may hold values from -0.25 to 0.25
Outputs:
- attention_out: bfloat16 [64, 4, 7168], P('grp', None, 'seq'), parts along dimension 0
There are 8 independent parts, one for each index of `grp`. A program takes and returns all parts, laid end to end along the dimension named above; an argument that names none is the same for every part. Nothing has to cross between parts.
Inputs may be any that keep to these rules, and one draw needn't show every extreme that they name: `context_lengths`: in every draw one request holds exactly 32768 tokens.
All inputs are finite; a program needn't handle non-finite values.
Results may differ from a plain program's by a relative error of at most 0.0058.
Values sent between devices are 32-bit elements; how exact they have to be, the bound alone decides.
A program may use at most 128 MiB of HBM per device.

v0:
```python
import jax
import jax.numpy as jnp
from jax import lax
from jax.sharding import PartitionSpec as P

score_scale = 0.07216878364870323
empty_mark = -1e30


def shard_partial(queries, cache_rows, context_lengths, first_token, latent_width):
    query_count = queries.shape[1]
    shard_width = cache_rows.shape[1]
    scores = (
        jnp.einsum("bqhc,btc->bqht", queries, cache_rows, preferred_element_type=jnp.float32)
        * score_scale
    )
    position = first_token + jnp.arange(shard_width, dtype=jnp.int32)
    row_limit = (
        context_lengths[:, None]
        - (query_count - 1)
        + jnp.arange(query_count, dtype=jnp.int32)[None, :]
    )
    visible = position[None, None, None, :] < row_limit[:, :, None, None]
    masked = jnp.where(visible, scores, empty_mark)
    row_peak = jnp.max(masked, axis=3)
    weights = jnp.where(visible, jnp.exp(masked - row_peak[..., None]), 0.0)
    row_rescale = jnp.maximum(jnp.sum(weights, axis=3), 1.0)
    values = jnp.einsum(
        "bqht,btc->bqhc",
        weights.astype(jnp.bfloat16),
        cache_rows[:, :, :latent_width],
        preferred_element_type=jnp.float32,
    )
    return (values / row_rescale[..., None], row_peak + jnp.log(row_rescale))


def combine_all(partials, log_sums):
    greatest_score = jnp.max(log_sums, axis=0)
    shares = jnp.exp(log_sums - greatest_score[None])
    return jnp.sum(shares[..., None] * partials, axis=0) / jnp.sum(shares, axis=0)[..., None]


def project_heads(attended, value_up, output_projection_rows):
    attended_low = attended.astype(jnp.bfloat16)
    head_out = jnp.einsum(
        "bqhc,hcv->bqhv", attended_low, value_up, preferred_element_type=jnp.float32
    ).astype(jnp.bfloat16)
    flattened_heads = head_out.reshape(head_out.shape[0], head_out.shape[1], -1)
    return jnp.einsum(
        "msp,pc->msc", flattened_heads, output_projection_rows, preferred_element_type=jnp.float32
    )


def local(queries, latent_cache, context_lengths, value_up, output_projection_rows):
    latent_width = value_up.shape[1]
    first_token = lax.axis_index("seq") * latent_cache.shape[1]
    partials, log_sums = shard_partial(
        queries, latent_cache, context_lengths, first_token, latent_width
    )
    term = project_heads(
        combine_all(
            lax.all_to_all(partials[None], "seq", split_axis=3, concat_axis=0, tiled=True),
            lax.all_to_all(log_sums[None], "seq", split_axis=3, concat_axis=0, tiled=True),
        ),
        value_up,
        output_projection_rows,
    )
    return lax.psum_scatter(term, "seq", scatter_dimension=2, tiled=True).astype(jnp.bfloat16)


def solution(mesh):
    placed = (
        P("grp", None, None, None),
        P("grp", "seq", None),
        P("grp"),
        P("seq", None, None),
        P("seq", None),
    )
    return jax.shard_map(
        local, mesh=mesh, in_specs=placed, out_specs=P("grp", None, "seq"), check_vma=False
    )
```

profile of v0, /device:TPU:1, one launch (start us, length us, event | category | flops | bytes accessed | tf_op | source)
XLA Modules:
  0.0 235.0 jit_solution(2712613659915861873)
XLA Ops:
  6.5 0.8 broadcast_add_fusion
  7.4 0.1 broadcast_compare_fusion
  7.5 0.8 copy-done
  8.3 6.3 %fusion.5 = (f32[8,4,64]{2,1,0:T(4,128)S(1)}, f32[8,4,64,1024]{3,2,1,0:T(8,128)S(1)}) fusion(pred[8,4,1024]{2,1,0:T(4,128)(4,1)S(1)} %broadcast_compare_fusion, bf16[8,4,64,576]{3,2,1,0:T(8,128)(2,1)S(1)} %copy-done, bf16[8,1024,576]{1,2,0:T(8,128)(2,1)} %param.6), kind=kOutput, calls=%fused_computation.7 | convolution fusion | flops 2422208512 | bytes 20226048 | tf_op jit(solution)/shard_map/bqhc,btc->bqht/dot_general | solution.py:14
  14.6 3.2 %copy-done.1 = f32[8,4,64,1024]{3,2,1,0:T(8,128)} copy-done((f32[8,4,64,1024]{3,2,1,0:T(8,128)}, f32[8,4,64,1024]{3,2,1,0:T(8,128)S(1)}, u32[]{:S(2)}) %copy-start.1) | copy-done | bytes 8388632
  17.8 2.8 %fusion.7 = f32[8,4,64]{2,1,0:T(4,128)S(1)} fusion(f32[8,4,64,1024]{3,2,1,0:T(8,128)S(1)} %get-tuple-element.10, f32[8,4,64]{2,1,0:T(4,128)S(1)} %get-tuple-element.9, pred[8,4,1024]{2,1,0:T(4,128)(4,1)S(1)} %broadcast_compare_fusion), kind=kLoop, calls=%fused_computation.9 | loop fusion | flops 10483712 | bytes 8437760 | tf_op jit(solution)/shard_map/reduce_sum | solution.py:27
  20.6 0.8 copy.24
  21.4 8.6 %all-to-all-start = ((f32[1,8,4,64]{1,2,0,3:T(4,128)}), f32[1,8,4,64]{1,2,0,3:T(4,128)S(1)}, u32[]{:S(2)}, u32[]{:S(2)}) async-start(f32[1,8,4,64]{1,2,0,3:T(4,128)} %copy.24), calls=%async_computation | async-start | bytes 262144 | tf_op jit(solution)/shard_map/all_to_all | solution.py:63
  30.0 10.7 %divide_bitcast_fusion = f32[1,8,4,64,512]{4,3,2,1,0:T(8,128)} fusion(f32[8,4,64]{2,1,0:T(4,128)S(1)} %get-tuple-element.8, bf16[8,1024,576]{1,2,0:T(8,128)(2,1)} %param.6, f32[8,4,64,1024]{3,2,1,0:T(8,128)} %copy-done.1, f32[8,4,64]{2,1,0:T(4,128)S(1)} %get-tuple-element.9, pred[8,4,1024]{2,1,0:T(4,128)(4,1)S(1)} %broadcast_compare_fusion), kind=kOutput, calls=%fused_computation.12 | convolution fusion | flops 2159017984 | bytes 21020672 | tf_op jit(solution)/shard_map/bqht,btc->bqhc/dot_general | solution.py:28
  40.7 6.8 %copy.28 = f32[1,8,4,64,512]{4,2,1,0,3:T(4,128)} copy(f32[1,8,4,64,512]{4,3,2,1,0:T(8,128)} %divide_bitcast_fusion) | data formatting | bytes 8388608 | tf_op jit(solution)/shard_map/broadcast_in_dim | solution.py:62
  47.5 7.6 %all-to-all-start.1 = ((f32[1,8,4,64,512]{4,2,1,0,3:T(4,128)}), f32[1,8,4,64,512]{4,2,1,0,3:T(4,128)}, u32[]{:S(2)}, u32[]{:S(2)}) async-start(f32[1,8,4,64,512]{4,2,1,0,3:T(4,128)} %copy.28), calls=%async_computation.1 | async-start | bytes 8388608 | tf_op jit(solution)/shard_map/all_to_all | solution.py:62
  55.1 0.2 reduce-scatter.4.cloned.1.call-start
  55.4 0.1 fusion.30
  55.5 0.8 copy.26
  56.3 49.0 %all-to-all-done.1 = f32[1,8,4,64,512]{4,2,1,0,3:T(4,128)} async-done(((f32[1,8,4,64,512]{4,2,1,0,3:T(4,128)}), f32[1,8,4,64,512]{4,2,1,0,3:T(4,128)}, u32[]{:S(2)}, u32[]{:S(2)}) %all-to-all-start.1) | async-done | bytes 4194336 | tf_op jit(solution)/shard_map/all_to_all | solution.py:62
  105.3 7.9 %fusion.9 = f32[8,4,2,512]{3,2,1,0:T(2,128)S(1)} fusion(f32[1,8,4,32,2,512]{5,2,1,4,3,0:T(4,128)} %bitcast.10, f32[32,8,4,2]{3,0,2,1:T(8,128)S(1)} %copy.26), kind=kLoop, calls=%fused_computation.11 | loop fusion | flops 2064384 | bytes 4333568 | tf_op jit(solution)/shard_map/reduce_sum | solution.py:40
  113.3 0.2 fusion.17
  113.5 2.8 %fusion.15 = f32[8,4,7168]{2,0,1:T(8,128)S(1)} fusion(bf16[256,7168]{1,0:T(8,128)(2,1)} %param.9, bf16[2,4,1,8,128]{4,3,2,1,0:T(8,128)(2,1)S(1)} %fusion.17), kind=kOutput, calls=%fused_computation.18 | convolution fusion | flops 117440512 | bytes 4603904 | tf_op jit(solution)/shard_map/msp,pc->msc/dot_general | solution.py:49
  116.3 9.4 %copy.37 = f32[8,4,7168]{0,1,2:T(4,128)} copy(f32[8,4,7168]{2,0,1:T(8,128)S(1)} %fusion.15) | data formatting | bytes 1835008
  125.6 12.0 %reshape.73 = f32[7168,32]{1,0:T(8,128)} reshape(f32[7168,4,8]{2,1,0:T(4,128)} %bitcast.49) | data formatting | bytes 1835008
  137.7 88.6 %reduce-scatter.4.cloned.1.call-done = f32[224,32]{1,0:T(8,128)} async-done(((f32[7168,32]{1,0:T(8,128)}), f32[224,32]{1,0:T(8,128)}) %reduce-scatter.4.cloned.1.call-update) | async-done | bytes 28688
  226.3 1.1 reshape.74
  227.4 0.1 copy.38
  227.5 0.6 copy.33
  (11 shorter events, 0.2 us)
Async XLA Ops:
  6.5 1.8 copy-start
  14.6 3.2 %copy-start.1 = (f32[8,4,64,1024]{3,2,1,0:T(8,128)}, f32[8,4,64,1024]{3,2,1,0:T(8,128)S(1)}, u32[]{:S(2)}) copy-start(f32[8,4,64,1024]{3,2,1,0:T(8,128)S(1)} %get-tuple-element.10) | copy-start | bytes 25165828
  21.4 26.1 %all-to-all-start = ((f32[1,8,4,64]{1,2,0,3:T(4,128)}), f32[1,8,4,64]{1,2,0,3:T(4,128)S(1)}, u32[]{:S(2)}, u32[]{:S(2)}) async-start(f32[1,8,4,64]{1,2,0,3:T(4,128)} %copy.24), calls=%async_computation | async-start | bytes 262144 | tf_op jit(solution)/shard_map/all_to_all | solution.py:63
  47.5 65.8 %copy-start.2 = (bf16[2,512,128]{2,1,0:T(8,128)(2,1)S(1)}, bf16[2,512,128]{2,1,0:T(8,128)(2,1)}, u32[]{:S(2)}) copy-start(bf16[2,512,128]{2,1,0:T(8,128)(2,1)} %param.8) | copy-start | bytes 786436
  47.5 57.8 %all-to-all-start.1 = ((f32[1,8,4,64,512]{4,2,1,0,3:T(4,128)}), f32[1,8,4,64,512]{4,2,1,0,3:T(4,128)}, u32[]{:S(2)}, u32[]{:S(2)}) async-start(f32[1,8,4,64,512]{4,2,1,0,3:T(4,128)} %copy.28), calls=%async_computation.1 | async-start | bytes 8388608 | tf_op jit(solution)/shard_map/all_to_all | solution.py:62
  55.1 171.2 %reduce-scatter.4.cloned.1.call-start = ((), (), s32[]{:S(2)}) async-start(), calls=%async_computation.3 | async-start | bytes 3784704
Sparse Core Ops, SparseCore 0:
  137.8 88.4 reduce-scatter.3
where the time goes:
time: 236 us; the launch traced here: 235 us
  waiting for transfers between devices  138 us (58%)
  local copies, waits for them, and re-layouts  35.6 us (15%)
  matrix products  20 us (8%)
  starting transfers between devices  16.4 us (7%)
  between operations  13.5 us (6%)
  other arithmetic  11.9 us (5%)
    unnamed x2, waiting for transfers between devices  88.6 us
    all_to_all x1, waiting for transfers between devices, local(): lax.all_to_all(partials[None], 'seq', split_axis=3, concat_axis=0, tiled=...  49 us
    unnamed x10, local copies, waits for them, and re-layouts  26.6 us
    dot_general x1, matrix products, shard_partial(): jnp.einsum('bqht,btc->bqhc', weights.astype(jnp.bfloat16), cache_rows[:,...  10.7 us
    all_to_all x1, starting transfers between devices, local(): lax.all_to_all(log_sums[None], 'seq', split_axis=3, concat_axis=0, tiled=...  8.6 us
    reduce_sum x1, other arithmetic, combine_all(): jnp.sum(shares[..., None] * partials, axis=0)  7.94 us
    all_to_all x1, starting transfers between devices, local(): lax.all_to_all(partials[None], 'seq', split_axis=3, concat_axis=0, tiled=...  7.55 us
    broadcast_in_dim x1, local copies, waits for them, and re-layouts, local(): partials[None]  6.81 us
  transfers between devices with their start and end apart: 3, of which 2 were waited for; matrix products, arithmetic and copies ran while one was open for 8% of the time, Pallas kernels for 0%

commit v1 on v0

v1 whole, which is shorter than its diff:
```python
import functools

import jax
import jax.numpy as jnp
from jax import lax
from jax.experimental import pallas as pl
from jax.experimental.pallas import tpu as pltpu
from jax.sharding import PartitionSpec as P

MESH = pl.DeviceIdType.MESH
f32, bf16 = jnp.float32, jnp.bfloat16

B, NQ, H, T, C, L, V, D = 8, 4, 64, 1024, 576, 512, 128, 7168
ROWS = NQ * H
DEV_COLS = D // 32
C2 = 0.07216878364870323 * 1.4426950408889634
EMPTY = -1e30
TICK_D, TICK_E = 4, 7


def iota(shape, dim):
    return lax.broadcasted_iota(jnp.int32, shape, dim)


def column(tile, lane):
    return jnp.broadcast_to(tile[:, lane : lane + 1], (8, 128))


def kernel(
    q_hbm, k_hbm, ctx_ref, vu_hbm, w_hbm, o_ref,
    q, k, vu, w, perm,
    cs, cr, p1, p1r, p2, p2r, att, ys, yr, z1r, z2, z2r,
    lsem, cs_s, cs_r, p1_s, p1_r, p2_s, p2_r, y_s, y_r, z1_s, z1_r, z2_s, z2_r,
):
    me = lax.axis_index("seq")
    c, x, y = me % 2, (me // 2) % 4, me // 8

    def device(yy, xx, cc):
        return (yy * 4 + xx) * 2 + cc

    other = device(y, x, 1 - c)

    def along(par, r):
        return device((y + r * par) % 4, (x + r * (1 - par)) % 4, c)

    barrier = pltpu.get_barrier_semaphore()
    partners = [other] + [along(par, r) for par in (0, 1) for r in (1, 2, 3)]
    for to in partners:
        pl.semaphore_signal(barrier, inc=1, device_id={"seq": to}, device_id_type=MESH)

    def load_q(b):
        return pltpu.make_async_copy(q_hbm.at[b], q.at[b], lsem.at[0, b])

    def load_k(b):
        return pltpu.make_async_copy(k_hbm.at[b], k.at[b], lsem.at[1, b])

    load_vu = pltpu.make_async_copy(vu_hbm, vu, lsem.at[2, 0])
    load_w = pltpu.make_async_copy(w_hbm, w, lsem.at[2, 1])
    for b in range(B):
        load_q(b).start()
        load_k(b).start()
    load_vu.start()
    load_w.start()

    row, col = iota((ROWS, ROWS), 0), iota((ROWS, ROWS), 1)
    r2, r1, cc = (row >> 3) & 3, (row >> 5) & 3, (row >> 7) & 1
    for par in (0, 1):
        rx, ry = (r1, r2) if par == 0 else (r2, r1)
        chip = ((y + ry) & 3) * 4 + ((x + rx) & 3)
        head = (chip * 2 + ((c + cc) & 1)) * 2 + ((row >> 2) & 1)
        perm[par] = jnp.where(col == (row & 3) * H + head, 1.0, 0.0).astype(bf16)

    pl.semaphore_wait(barrier, len(partners))

    lane = iota((8, 128), 1)

    def remote(src, dst, ssem, rsem, to):
        return pltpu.make_async_remote_copy(
            src_ref=src, dst_ref=dst, send_sem=ssem, recv_sem=rsem,
            device_id={"seq": to}, device_id_type=MESH,
        )

    def copy_c(b):
        return remote(cs.at[b], cr.at[b], cs_s.at[b], cs_r.at[b], other)

    def copy_p1(b, r):
        return remote(
            p1.at[b, r], p1r.at[b, r - 1], p1_s.at[b, r - 1], p1_r.at[b, r - 1], along(b % 2, r)
        )

    def copy_p2(b, r):
        return remote(
            p2.at[b, r], p2r.at[b, r - 1], p2_s.at[b, r - 1], p2_r.at[b, r - 1], along(1 - b % 2, r)
        )

    def attend(b):
        load_q(b).wait()
        load_k(b).wait()
        queries = jnp.dot(perm[b % 2], q[b], preferred_element_type=f32).astype(bf16)
        s = jnp.dot(queries, k[b], preferred_element_type=f32)
        limit = (ctx_ref[b] - (NQ - 1) - me * T) + (iota((ROWS, 1), 0) & 3)
        s = jnp.where(iota((ROWS, T), 1) < limit, s, EMPTY)
        peak = jnp.max(s, axis=1, keepdims=True)
        e = jnp.exp2((s - peak) * C2)
        total = jnp.sum(e, axis=1, keepdims=True)
        acc = lax.dot_general(
            e.astype(bf16), k[b, :L, :], (((1,), (1,)), ((), ())), preferred_element_type=f32
        )
        peak = peak * C2
        for half, ref in ((0, p1), (1, cs)):
            for g in range(4):
                stat = jnp.zeros((8, 128), f32)
                for t in range(4):
                    at = ((half * 4 + g) * 4 + t) * 8
                    stat = jnp.where(lane == t, peak[at : at + 8], stat)
                    stat = jnp.where(lane == 64 + t, total[at : at + 8], stat)
                    for i in range(4):
                        ref[b, g, t * 4 + i] = acc[at : at + 8, i * 128 : i * 128 + 128]
                ref[b, g, 16] = stat
        copy_c(b).start()

    def merge_stats(stats):
        top = functools.reduce(jnp.maximum, stats)
        shares = [jnp.exp2(s - top) for s in stats]
        total = sum(pltpu.roll(f, 64, 1) * s for f, s in zip(shares, stats))
        return shares, jnp.where(lane < 64, top, total)

    def merge_core(b):
        copy_c(b).wait_recv()
        for g in range(4):
            shares, stat = merge_stats([p1[b, g, 16], cr[b, g, 16]])
            for t in range(4):
                f0, f1 = column(shares[0], t), column(shares[1], t)
                for i in range(4):
                    at = t * 4 + i
                    p1[b, g, at] = f0 * p1[b, g, at] + f1 * cr[b, g, at]
            p1[b, g, 16] = stat
        for r in (1, 2, 3):
            copy_p1(b, r).start()

    def merge_first(b):
        for r in (1, 2, 3):
            copy_p1(b, r).wait_recv()
        parts = [p1.at[b, 0]] + [p1r.at[b, r] for r in range(3)]
        shares, stat = merge_stats([part[16] for part in parts])
        for t in range(4):
            f = [column(s, t) for s in shares]
            for i in range(4):
                p2[b, t, i] = sum(f[n] * parts[n][t * 4 + i] for n in range(4))
            p2[b, t, 4] = stat
        for r in (1, 2, 3):
            copy_p2(b, r).start()

    def merge_second(b):
        for r in (1, 2, 3):
            copy_p2(b, r).wait_recv()
        parts = [p2.at[b, 0]] + [p2r.at[b, r] for r in range(3)]
        peaks = [column(part[4], t) for t, part in enumerate(parts)]
        totals = [column(part[4], 64 + t) for t, part in enumerate(parts)]
        top = functools.reduce(jnp.maximum, peaks)
        f = [jnp.exp2(p - top) for p in peaks]
        inverse = 1.0 / sum(a * b for a, b in zip(f, totals))
        for i in range(4):
            att[b, :, i * 128 : i * 128 + 128] = sum(f[n] * parts[n][i] for n in range(4)) * inverse

    def tick(i, _):
        @pl.when(i < B)
        def _():
            attend(i)

        @pl.when((i >= 1) & (i < B + 1))
        def _():
            merge_core(i - 1)

        @pl.when((i >= TICK_D) & (i < B + TICK_D))
        def _():
            merge_first(i - TICK_D)

        @pl.when((i >= TICK_E) & (i < B + TICK_E))
        def _():
            merge_second(i - TICK_E)

        return 0

    lax.fori_loop(0, B + TICK_E, tick, 0)

    load_vu.wait()
    load_w.wait()
    low = att[...].reshape(B * 8, L).astype(bf16)
    up = [jnp.dot(low, vu[n], preferred_element_type=f32) for n in range(2)]
    sub = iota((8, 128), 0)
    rows = []
    for b in range(0, B, 2):
        a = [up[n][8 * b : 8 * b + 8] for n in range(2)]
        z = [up[n][8 * b + 8 : 8 * b + 16] for n in range(2)]
        h0 = jnp.where(sub < 4, a[0], pltpu.roll(z[0], 4, 0))
        h1 = jnp.where(sub < 4, pltpu.roll(a[1], 4, 0), z[1])
        rows.append(jnp.concatenate([h0, h1], axis=1))
    head_out = jnp.concatenate(rows, axis=0).astype(bf16)

    def copy_y(part):
        return remote(ys.at[1 - c, part], yr.at[part], y_s.at[part], y_r.at[part], other)

    mine = (x, y)

    def copy_z1(part, r):
        return remote(
            ys.at[c, part, (mine[part] + r) % 4], z1r.at[part, r - 1],
            z1_s.at[part, r - 1], z1_r.at[part, r - 1], along(part, r),
        )

    def copy_z2(part, r):
        return remote(
            z2.at[part, (mine[1 - part] + r) % 4], z2r.at[part, r - 1],
            z2_s.at[part, r - 1], z2_r.at[part, r - 1], along(1 - part, r),
        )

    for four in range(8):
        out = jnp.dot(head_out, w[:, four * 896 : four * 896 + 896], preferred_element_type=f32)
        for dev in range(4):
            start = dev * DEV_COLS
            low_tile = start // 128 * 128
            wide = out[:, low_tile : min(low_tile + 384, 896)]
            width = wide.shape[1]
            if start != low_tile:
                wide = pltpu.roll(wide, width - (start - low_tile), 1)
            chip = four * 2 + dev // 2
            yy, xx = chip // 4, chip % 4
            for part in range(2):
                first, second = (xx, yy) if part == 0 else (yy, xx)
                for rt in range(2):
                    for i in range(2):
                        ys[dev % 2, part, first, second, rt * 2 + i] = wide[
                            part * 16 + rt * 8 : part * 16 + rt * 8 + 8, i * 128 : i * 128 + 128
                        ]
    for part in range(2):
        copy_y(part).start()
    for part in range(2):
        copy_y(part).wait_recv()
        for first in range(4):
            ys[c, part, first] = ys[c, part, first] + yr[part, first]
        for r in (1, 2, 3):
            copy_z1(part, r).start()
    for part in range(2):
        for r in (1, 2, 3):
            copy_z1(part, r).wait_recv()
        z2[part] = ys[c, part, mine[part]] + z1r[part, 0] + z1r[part, 1] + z1r[part, 2]
        for r in (1, 2, 3):
            copy_z2(part, r).start()
    for part in range(2):
        for r in (1, 2, 3):
            copy_z2(part, r).wait_recv()
        done = z2[part, mine[1 - part]] + z2r[part, 0] + z2r[part, 1] + z2r[part, 2]
        for rt in range(2):
            tile = jnp.concatenate([done[rt * 2], done[rt * 2 + 1]], axis=1)[:, :DEV_COLS]
            at = part * 16 + rt * 8
            o_ref[at : at + 8, :] = tile

    def drain(b, _):
        copy_c(b).wait_send()
        for r in (1, 2, 3):
            copy_p1(b, r).wait_send()
            copy_p2(b, r).wait_send()
        return 0

    lax.fori_loop(0, B, drain, 0)
    for part in range(2):
        copy_y(part).wait_send()
        for r in (1, 2, 3):
            copy_z1(part, r).wait_send()
            copy_z2(part, r).wait_send()


def local(queries, latent_cache, context_lengths, value_up, output_projection_rows):
    tile = (8, 128)
    dma = pltpu.SemaphoreType.DMA
    out = pl.pallas_call(
        kernel,
        out_shape=jax.ShapeDtypeStruct((B * NQ, DEV_COLS), f32),
        in_specs=[
            pl.BlockSpec(memory_space=pl.ANY),
            pl.BlockSpec(memory_space=pl.ANY),
            pl.BlockSpec(memory_space=pltpu.SMEM),
            pl.BlockSpec(memory_space=pl.ANY),
            pl.BlockSpec(memory_space=pl.ANY),
        ],
        out_specs=pl.BlockSpec(memory_space=pltpu.VMEM),
        scratch_shapes=[
            pltpu.VMEM((B, ROWS, C), bf16),
            pltpu.VMEM((B, C, T), bf16),
            pltpu.VMEM((2, L, V), bf16),
            pltpu.VMEM((2 * V, D), bf16),
            pltpu.VMEM((2, ROWS, ROWS), bf16),
            pltpu.VMEM((B, 4, 17) + tile, f32),
            pltpu.VMEM((B, 4, 17) + tile, f32),
            pltpu.VMEM((B, 4, 17) + tile, f32),
            pltpu.VMEM((B, 3, 17) + tile, f32),
            pltpu.VMEM((B, 4, 5) + tile, f32),
            pltpu.VMEM((B, 3, 5) + tile, f32),
            pltpu.VMEM((B, 8, L), f32),
            pltpu.VMEM((2, 2, 4, 4, 4) + tile, f32),
            pltpu.VMEM((2, 4, 4, 4) + tile, f32),
            pltpu.VMEM((2, 3, 4, 4) + tile, f32),
            pltpu.VMEM((2, 4, 4) + tile, f32),
            pltpu.VMEM((2, 3, 4) + tile, f32),
            dma((3, B)),
            dma((B,)), dma((B,)),
            dma((B, 3)), dma((B, 3)),
            dma((B, 3)), dma((B, 3)),
            dma((2,)), dma((2,)),
            dma((2, 3)), dma((2, 3)),
            dma((2, 3)), dma((2, 3)),
        ],
        compiler_params=pltpu.CompilerParams(
            collective_id=0, has_side_effects=True, vmem_limit_bytes=56 * 2**20
        ),
        name="attend_and_project",
    )(
        queries.reshape(B, ROWS, C),
        jnp.swapaxes(latent_cache, 1, 2),
        context_lengths,
        value_up,
        output_projection_rows,
    )
    return out.reshape(B, NQ, DEV_COLS).astype(bf16)


def solution(mesh):
    placed = (
        P("grp", None, None, None),
        P("grp", "seq", None),
        P("grp"),
        P("seq", None, None),
        P("seq", None),
    )
    return jax.shard_map(
        local, mesh=mesh, in_specs=placed, out_specs=P("grp", None, "seq"), check_vma=False
    )
```

time: 236 us -> 46.1 us (0.20)
  waiting for transfers between devices: 138 us -> 0 us
  Pallas kernels: 0 us -> 44.5 us
  local copies, waits for them, and re-layouts: 35.6 us -> 0.62 us
  matrix products: 20 us -> 0 us
  starting transfers between devices: 16.4 us -> 0 us
  between operations: 13.5 us -> 0.01 us
  other arithmetic: 11.9 us -> 0.76 us
    unnamed x2 -> x0, waiting for transfers between devices: 88.6 us -> none
    all_to_all x2 -> x0, waiting for transfers between devices: 49 us -> none  [the longest x1 49 us: local(): lax.all_to_all(partials[None], 'seq', split_axis=3, concat_axis=0, tiled=...]
    pallas_call x0 -> x1, Pallas kernels: none -> 44.5 us  [local(): pl.pallas_call(kernel, out_shape=jax.ShapeDtypeStruct((B * NQ, DEV_COLS),...]
    unnamed x10 -> x0, local copies, waits for them, and re-layouts: 26.6 us -> none
    dot_general x4 -> x0, matrix products: 20 us -> none  [the longest x1 10.7 us: shard_partial(): jnp.einsum('bqht,btc->bqhc', weights.astype(jnp.bfloat16), cache_rows[:,...]
    all_to_all x2 -> x0, starting transfers between devices: 16.2 us -> none  [the longest x1 8.6 us: local(): lax.all_to_all(log_sums[None], 'seq', split_axis=3, concat_axis=0, tiled=...]
    reduce_sum x3 -> x0, other arithmetic: 10.9 us -> none  [the longest x1 7.94 us: combine_all(): jnp.sum(shares[..., None] * partials, axis=0)]
    broadcast_in_dim x1 -> x0, local copies, waits for them, and re-layouts: 6.81 us -> none  [local(): partials[None]]
  transfers between devices with their start and end apart: 3 -> 0, of which waited for: 2 -> 0; matrix products, arithmetic and copies ran while one was open for 8% -> 0% of each run, Pallas kernels for 0% -> 0%
where the time goes in v1:
time: 46.1 us; the launch traced here: 45.9 us
  Pallas kernels  44.5 us (97%)
  other arithmetic  0.76 us (2%)
  local copies, waits for them, and re-layouts  0.62 us (1%)
    pallas_call x1, Pallas kernels, local(): pl.pallas_call(kernel, out_shape=jax.ShapeDtypeStruct((B * NQ, DEV_COLS),...  44.5 us

profile of v1, /device:TPU:1, one launch (start us, length us, event | category | flops | bytes accessed | tf_op | source)
XLA Modules:
  0.0 45.9 jit_solution(18364996745217800762)
XLA Ops:
  0.0 44.5 %attend_and_project.1 = f32[32,224]{1,0:T(8,128)} custom-call(bf16[8,256,576]{2,1,0:T(8,128)(2,1)} %bitcast.3, bf16[8,576,1024]{2,1,0:T(8,128)(2,1)} %bitcast.2, s32[8]{0:T(128)} %ctx_ref.1, bf16[2,512,128]{2,1,0:T(8,128)(2,1)} %vu_hbm.1, bf16[256,7168]{1,0:T(8,128)(2,1)} %w_hbm.1), custom_call_target="tpu_custom_call" | custom-call | tf_op jit(solution)/shard_map/attend_and_project/pallas_call | solution.py:277
  44.5 0.8 %convert_element_type.6 = bf16[32,224]{1,0:T(8,128)(2,1)S(1)} convert(f32[32,224]{1,0:T(8,128)} %attend_and_project.1) | non-fusion elementwise | flops 7168 | bytes 43008 | tf_op jit(solution)/shard_map/convert_element_type | solution.py:325
  45.3 0.6 %convert_element_type.7 = bf16[8,4,224]{2,1,0:T(4,128)(2,1)} reshape(bf16[32,224]{1,0:T(8,128)(2,1)S(1)} %convert_element_type.6) | data formatting | bytes 28672 | tf_op jit(solution)/shard_map/convert_element_type | solution.py:325

commit v2 on v1

v2 whole, which is shorter than its diff:
```python
import functools

import jax
import jax.numpy as jnp
from jax import lax
from jax.experimental import pallas as pl
from jax.experimental.pallas import tpu as pltpu
from jax.sharding import PartitionSpec as P

MESH = pl.DeviceIdType.MESH
f32, bf16 = jnp.float32, jnp.bfloat16

B, NQ, H, T, C, L, V, D = 8, 4, 64, 1024, 576, 512, 128, 7168
ROWS = NQ * H
DEV_COLS = D // 32
C2 = 0.07216878364870323 * 1.4426950408889634
EMPTY = -1e30
TICK_R, TICK_D = 3, 6
RELAYED = 6
GROUPS = ((0, 4), (4, 8))
CHIPS = sorted(
    [(dx, dy) for dy in range(4) for dx in range(4) if dx or dy],
    key=lambda o: -(min(o[0], 4 - o[0]) + min(o[1], 4 - o[1])),
)


def iota(shape, dim):
    return lax.broadcasted_iota(jnp.int32, shape, dim)


def column(tile, lane):
    return jnp.broadcast_to(tile[:, lane : lane + 1], (8, 128))


def blocks_transposed(tiles):
    sub = iota((8, 128), 0)
    low, even = sub < 4, (sub & 2) == 0
    half = [pltpu.roll(t, 4, 0) for t in tiles]
    a0, a2 = jnp.where(low, tiles[0], half[2]), jnp.where(low, half[0], tiles[2])
    a1, a3 = jnp.where(low, tiles[1], half[3]), jnp.where(low, half[1], tiles[3])
    out = []
    for p, r in ((a0, a1), (a2, a3)):
        out.append(jnp.where(even, p, pltpu.roll(r, 2, 0)))
        out.append(jnp.where(even, pltpu.roll(p, 6, 0), r))
    return out


def tile_at(second, part):
    return second * 4 + part + second // 2


def head_major(tile):
    sub = iota((8, 128), 0)
    out = tile
    for to, at in ((1, 2), (2, 4), (3, 6), (4, 1), (5, 3), (6, 5)):
        out = jnp.where(sub == to, pltpu.roll(tile, (to - at) % 8, 0), out)
    return out


def kernel(
    q_hbm, k_hbm, ctx_ref, vu_hbm, w_hbm, o_ref,
    q, k, vu, w, sc, pk,
    pc, cr, mg, rr, p1r, p2, p2r, att,
    lsem, cs_s, cs_r, r_s, r_r, p1_s, p1_r, p2_s, p2_r, y_s, y_r, z_s, z_r, *terms
):
    me = lax.axis_index("seq")
    c, x, y = me % 2, (me // 2) % 4, me // 8

    def device(yy, xx, cc):
        return (yy * 4 + xx) * 2 + cc

    other = device(y, x, 1 - c)

    def along(par, r):
        return device((y + r * par) % 4, (x + r * (1 - par)) % 4, c)

    def position(par):
        return x + (y - x) * par

    barrier = pltpu.get_barrier_semaphore()
    def chip_at(offset):
        return ((y + offset[1]) % 4) * 4 + (x + offset[0]) % 4

    partners = [other] + [along(par, r) for par in (0, 1) for r in (1, 2, 3)]
    for to in partners:
        pl.semaphore_signal(barrier, inc=1, device_id={"seq": to}, device_id_type=MESH)

    def load_q(b):
        return pltpu.make_async_copy(q_hbm.at[b], q.at[b], lsem.at[0, b])

    def load_k(b):
        return pltpu.make_async_copy(k_hbm.at[b], k.at[b], lsem.at[1, b])

    load_vu = pltpu.make_async_copy(vu_hbm, vu, lsem.at[2, 0])
    load_w = pltpu.make_async_copy(w_hbm, w, lsem.at[2, 1])
    for b in range(B):
        load_q(b).start()
        load_k(b).start()
    load_vu.start()
    load_w.start()

    lane = iota((8, 128), 1)

    def remote(src, dst, ssem, rsem, to):
        return pltpu.make_async_remote_copy(
            src_ref=src, dst_ref=dst, send_sem=ssem, recv_sem=rsem,
            device_id={"seq": to}, device_id_type=MESH,
        )

    def copy_c(b):
        return remote(pc.at[b, 1 - c], cr.at[b], cs_s.at[b], cs_r.at[b], other)

    def copy_p1(b, r):
        return remote(
            mg.at[b, (position(b % 2) + r) % 4], p1r.at[b, r - 1],
            p1_s.at[b, r - 1], p1_r.at[b, r - 1], along(b % 2, r),
        )

    def copy_p2(b, r):
        return remote(
            p2.at[b, (position(1 - b % 2) + r) % 4], p2r.at[b, r - 1],
            p2_s.at[b, r - 1], p2_r.at[b, r - 1], along(1 - b % 2, r),
        )

    def scores(b, slot):
        load_q(b).wait()
        load_k(b).wait()
        s = jnp.dot(q[b], k[b], preferred_element_type=f32)
        limit = (ctx_ref[b] - (NQ - 1) - me * T) + (iota((ROWS, 1), 0) >> 6)
        s = jnp.where(iota((ROWS, T), 1) < limit, s, EMPTY)
        sc[slot] = s
        pk[slot] = jnp.broadcast_to(jnp.max(s, axis=1, keepdims=True), (ROWS, 128))

    def attend(b, slot, following=True):
        if following:
            scores(b + 1, 1 - slot)
        peak = pk[slot]
        e = jnp.exp2((sc[slot] - peak[:, :1]) * C2)
        total = jnp.sum(e, axis=1, keepdims=True)
        acc = lax.dot_general(
            e.astype(bf16), k[b, :L, :], (((1,), (1,)), ((), ())), preferred_element_type=f32
        )
        both = jnp.where(iota((ROWS, 128), 1) < 64, peak * C2, total)
        stats = {}
        for eight in range(8):
            rows = [slice(n * 64 + eight * 8, n * 64 + eight * 8 + 8) for n in range(4)]
            for part in range(5):
                src = both if part == 4 else acc[:, part * 128 : part * 128 + 128]
                for n, tile in enumerate(blocks_transposed([src[r] for r in rows])):
                    chip, core = (eight * 4 + n) // 2, n % 2
                    yy, xx = chip // 4, chip % 4
                    first, second = (xx, yy) if slot == 0 else (yy, xx)
                    if part < 4:
                        pc[b, core, first, tile_at(second, part)] = tile
                    else:
                        before = stats.get((core, first), jnp.zeros((8, 128), f32))
                        stats[core, first] = jnp.where((lane & 63) == second, tile, before)
        for (core, first), tile in stats.items():
            pc[b, core, first, 8] = tile

    def merge_stats(stats):
        top = functools.reduce(jnp.maximum, stats)
        shares = [jnp.exp2(s - top) for s in stats]
        total = sum(pltpu.roll(f, 64, 1) * s for f, s in zip(shares, stats))
        return shares, jnp.where(lane < 64, top, total)

    def merge_core(b):
        copy_c(b).wait_recv()
        merged = [merge_stats([pc[b, c, g, 8], cr[b, g, 8]]) for g in range(4)]
        for g in range(4):
            shares, stat = merged[g]
            for t in range(4):
                f0, f1 = column(shares[0], t), column(shares[1], t)
                for i in range(4):
                    at = tile_at(t, i)
                    mg[b, g, at] = f0 * pc[b, c, g, at] + f1 * cr[b, g, at]
            mg[b, g, 8] = stat

    def copy_r(b, way):
        par = b % 2
        return remote(
            mg.at[b, (position(par) + 2) % 4, pl.ds(8 * way, 9)], rr.at[b, way],
            r_s.at[b, way], r_r.at[b, way], along(par, 1 + 2 * way),
        )

    def start_relay(b):
        for way in range(2):
            copy_r(b, way).start()

    def relay(b):
        for way in range(2):
            copy_r(b, way).wait_recv()
        for way in range(2):
            g = (position(b % 2) + 1 + 2 * way) % 4
            mine = mg[b, g, 8]
            shares, stat = merge_stats([mine, rr[b, way, 8 - 8 * way]])
            for t in (2 * way, 2 * way + 1):
                f0, f1 = column(shares[0], t), column(shares[1], t)
                for i in range(4):
                    at = tile_at(t, i)
                    mg[b, g, at] = f0 * mg[b, g, at] + f1 * rr[b, way, at - 8 * way]
            mg[b, g, 8] = jnp.where((lane & 63) // 2 == way, stat, mine)
            copy_p1(b, 1 + 2 * way).start()

    def send_p1(b):
        for r in (2, 1, 3):
            copy_p1(b, r).start()

    def merge_first(b, relayed):
        steps = (1, 3) if relayed else (1, 2, 3)
        for r in steps:
            copy_p1(b, r).wait_recv()
        parts = [mg.at[b, position(b % 2)]] + [p1r.at[b, r - 1] for r in steps]
        shares, stat = merge_stats([part[8] for part in parts])
        for t in range(4):
            f = [column(s, t) for s in shares]
            for i in range(4):
                p2[b, t, i] = sum(f[n] * parts[n][tile_at(t, i)] for n in range(len(parts)))
            p2[b, t, 4] = pltpu.roll(stat, 128 - t, 1) if t else stat
        for r in (2, 1, 3):
            copy_p2(b, r).start()

    def merge_second(b):
        for r in (1, 2, 3):
            copy_p2(b, r).wait_recv()
        parts = [p2.at[b, position(1 - b % 2)]] + [p2r.at[b, r] for r in range(3)]
        peaks = [column(part[4], 0) for part in parts]
        totals = [column(part[4], 64) for part in parts]
        top = functools.reduce(jnp.maximum, peaks)
        f = [jnp.exp2(p - top) for p in peaks]
        inverse = 1.0 / sum(a * b for a, b in zip(f, totals))
        for i in range(4):
            tile = sum(f[n] * parts[n][i] for n in range(4)) * inverse
            att[b, :, i * 128 : i * 128 + 128] = head_major(tile)

    def before(i):
        merge_core(i - 1)
        start_relay(i - 1)

    def services(i):
        if isinstance(i, int):
            if i >= TICK_R:
                relay(i - TICK_R)
            if i >= TICK_D:
                merge_first(i - TICK_D, True)
            return

        @pl.when(i >= TICK_R)
        def _():
            relay(i - TICK_R)

    def pair(j, _):
        for slot in range(2):
            i = 2 * j + slot
            attend(i, slot)
            copy_c(i).start()
            before(i)
            services(i)
        return 0

    scores(0, 0)
    attend(0, 0)
    pl.semaphore_wait(barrier, len(partners))
    copy_c(0).start()
    attend(1, 1)
    copy_c(1).start()
    before(1)
    lax.fori_loop(1, B // 2 - 1, pair, 0)
    attend(B - 2, 0)
    copy_c(B - 2).start()
    before(B - 2)
    services(B - 2)
    attend(B - 1, 1, False)
    copy_c(B - 1).start()
    merge_core(B - 2)
    send_p1(B - 2)
    services(B - 1)

    def late_relay(b, _):
        relay(b)
        return 0

    def late_relayed(b, _):
        merge_first(b, True)
        return 0

    def late_direct(b, _):
        merge_first(b, False)
        return 0

    def late_second(b, _):
        merge_second(b)
        return 0

    def second(start, stop):
        lax.fori_loop(start, stop, late_second, 0)

    merge_core(B - 1)
    send_p1(B - 1)
    lax.fori_loop(B - TICK_R, RELAYED, late_relay, 0)
    lax.fori_loop(B - TICK_D, 4, late_relayed, 0)
    second(0, 2)
    lax.fori_loop(4, RELAYED, late_relayed, 0)
    lax.fori_loop(RELAYED, B, late_direct, 0)

    sub = iota((8, 128), 0)

    def copy_y(n):
        ys, yr, _ = terms[3 * n : 3 * n + 3]
        return remote(ys.at[1 - c], yr, y_s.at[n], y_r.at[n], other)

    def copy_z(n, to):
        ys, _, zr = terms[3 * n : 3 * n + 3]
        chip = chip_at(CHIPS[to])
        return remote(ys.at[c, chip], zr.at[to], z_s.at[n, to], z_r.at[n, to], chip * 2 + c)

    def project(n):
        lo, hi = GROUPS[n]
        ys = terms[3 * n]
        low = att[lo:hi].reshape((hi - lo) * 8, L).astype(bf16)
        up = [jnp.dot(low, vu[h], preferred_element_type=f32) for h in range(2)]
        rows = []
        for b in range(0, hi - lo, 2):
            a = [up[h][8 * b : 8 * b + 8] for h in range(2)]
            z = [up[h][8 * b + 8 : 8 * b + 16] for h in range(2)]
            h0 = jnp.where(sub < 4, a[0], pltpu.roll(z[0], 4, 0))
            h1 = jnp.where(sub < 4, pltpu.roll(a[1], 4, 0), z[1])
            rows.append(jnp.concatenate([h0, h1], axis=1))
        head_out = jnp.concatenate(rows, axis=0).astype(bf16)
        for four in range(8):
            out = jnp.dot(head_out, w[:, four * 896 : four * 896 + 896], preferred_element_type=f32)
            for dev in range(4):
                start = dev * DEV_COLS
                low_tile = start // 128 * 128
                wide = out[:, low_tile : min(low_tile + 384, 896)]
                width = wide.shape[1]
                if start != low_tile:
                    wide = pltpu.roll(wide, width - (start - low_tile), 1)
                for rt in range(len(rows)):
                    for i in range(2):
                        ys[dev % 2, four * 2 + dev // 2, rt * 2 + i] = wide[
                            rt * 8 : rt * 8 + 8, i * 128 : i * 128 + 128
                        ]
        copy_y(n).start()

    def spread(n):
        ys, yr, _ = terms[3 * n : 3 * n + 3]
        copy_y(n).wait_recv()
        for chip in range(16):
            ys[c, chip] = ys[c, chip] + yr[chip]
        for to in range(15):
            copy_z(n, to).start()

    def finish(n):
        lo, hi = GROUPS[n]
        ys, _, zr = terms[3 * n : 3 * n + 3]
        for to in range(15):
            copy_z(n, to).wait_recv()
        done = ys[c, chip_at((0, 0))]
        for to in range(15):
            done = done + zr[to]
        for rt in range((hi - lo) // 2):
            tile = jnp.concatenate([done[rt * 2], done[rt * 2 + 1]], axis=1)[:, :DEV_COLS]
            for half in range(2):
                o_ref[lo + rt * 2 + half] = tile[half * 4 : half * 4 + 4]

    load_vu.wait()
    load_w.wait()
    second(2, GROUPS[0][1])
    project(0)
    second(GROUPS[0][1], B - 2)
    spread(0)
    second(B - 2, B)
    project(1)
    spread(1)
    finish(0)
    finish(1)

    def drain(b, _):
        copy_c(b).wait_send()

        @pl.when(b < RELAYED)
        def _():
            for way in range(2):
                copy_r(b, way).wait_send()

        @pl.when(b >= RELAYED)
        def _():
            copy_p1(b, 2).wait_send()

        for r in (1, 3):
            copy_p1(b, r).wait_send()
        for r in (1, 2, 3):
            copy_p2(b, r).wait_send()
        return 0

    lax.fori_loop(0, B, drain, 0)
    for n in range(len(GROUPS)):
        copy_y(n).wait_send()
        for to in range(15):
            copy_z(n, to).wait_send()


def local(queries, latent_cache, context_lengths, value_up, output_projection_rows):
    tile = (8, 128)
    dma = pltpu.SemaphoreType.DMA
    out = pl.pallas_call(
        kernel,
        out_shape=pltpu.VMEM((B, NQ, DEV_COLS), f32),
        in_specs=[
            pl.BlockSpec(memory_space=pl.ANY),
            pl.BlockSpec(memory_space=pl.ANY),
            pl.BlockSpec(memory_space=pltpu.SMEM),
            pl.BlockSpec(memory_space=pl.ANY),
            pl.BlockSpec(memory_space=pl.ANY),
        ],
        out_specs=pl.BlockSpec(memory_space=pltpu.VMEM),
        scratch_shapes=[
            pltpu.VMEM((B, ROWS, C), bf16),
            pltpu.VMEM((B, C, T), bf16),
            pltpu.VMEM((2, L, V), bf16),
            pltpu.VMEM((2 * V, D), bf16),
            pltpu.VMEM((2, ROWS, T), f32),
            pltpu.VMEM((2, ROWS, 128), f32),
            pltpu.VMEM((B, 2, 4, 17) + tile, f32),
            pltpu.VMEM((B, 4, 17) + tile, f32),
            pltpu.VMEM((B, 4, 17) + tile, f32),
            pltpu.VMEM((B, 2, 9) + tile, f32),
            pltpu.VMEM((B, 3, 17) + tile, f32),
            pltpu.VMEM((B, 4, 5) + tile, f32),
            pltpu.VMEM((B, 3, 5) + tile, f32),
            pltpu.VMEM((B, 8, L), f32),
            dma((3, B)),
            dma((B,)), dma((B,)),
            dma((B, 2)), dma((B, 2)),
            dma((B, 3)), dma((B, 3)),
            dma((B, 3)), dma((B, 3)),
            dma((len(GROUPS),)), dma((len(GROUPS),)),
            dma((len(GROUPS), 15)), dma((len(GROUPS), 15)),
        ]
        + [
            pltpu.VMEM(lead + (hi - lo,) + tile, f32)
            for lo, hi in GROUPS
            for lead in ((2, 16), (16,), (15,))
        ],
        compiler_params=pltpu.CompilerParams(
            collective_id=0, has_side_effects=True, vmem_limit_bytes=56 * 2**20
        ),
        name="attend_and_project",
    )(
        queries.reshape(B, ROWS, C),
        jnp.swapaxes(latent_cache, 1, 2),
        context_lengths,
        value_up,
        output_projection_rows,
    )
    return out.astype(bf16)


def solution(mesh):
    placed = (
        P("grp", None, None, None),
        P("grp", "seq", None),
        P("grp"),
        P("seq", None, None),
        P("seq", None),
    )
    return jax.shard_map(
        local, mesh=mesh, in_specs=placed, out_specs=P("grp", None, "seq"), check_vma=False
    )
```

time: 46.1 us -> 41.9 us (0.909)
  Pallas kernels: 44.5 us -> 41.2 us
  local copies, waits for them, and re-layouts: 0.62 us -> 0 us
    pallas_call x1, Pallas kernels: 44.5 us -> 41.2 us  [local(): pl.pallas_call(kernel, out_shape=pltpu.VMEM((B, NQ, DEV_COLS), f32), in_s...]
    convert_element_type x1 -> x0, local copies, waits for them, and re-layouts: 0.62 us -> none  [local(): return out.reshape(B, NQ, DEV_COLS).astype(bf16)]
where the time goes in v2:
time: 41.9 us; the launch traced here: 41.8 us
  Pallas kernels  41.2 us (98%)
  other arithmetic  0.61 us (1%)
    pallas_call x1, Pallas kernels, local(): pl.pallas_call(kernel, out_shape=pltpu.VMEM((B, NQ, DEV_COLS), f32), in_s...  41.2 us

profile of v2, /device:TPU:1, one launch (start us, length us, event | category | flops | bytes accessed | tf_op | source)
XLA Modules:
  0.0 41.8 jit_solution(14737467128486374171)
XLA Ops:
  0.0 41.2 %attend_and_project.1 = f32[8,4,224]{2,1,0:T(4,128)S(1)} custom-call(bf16[8,256,576]{2,1,0:T(8,128)(2,1)} %bitcast.3, bf16[8,576,1024]{2,1,0:T(8,128)(2,1)} %bitcast.2, s32[8]{0:T(128)} %ctx_ref.1, bf16[2,512,128]{2,1,0:T(8,128)(2,1)} %vu_hbm.1, bf16[256,7168]{1,0:T(8,128)(2,1)} %w_hbm.1), custom_call_target="tpu_custom_call" | custom-call | tf_op jit(solution)/shard_map/attend_and_project/pallas_call | solution.py:407
  41.2 0.6 %convert_element_type.3 = bf16[8,4,224]{2,1,0:T(4,128)(2,1)} convert(f32[8,4,224]{2,1,0:T(4,128)S(1)} %attend_and_project.1) | non-fusion elementwise | flops 7168 | bytes 43008 | tf_op jit(solution)/shard_map/convert_element_type | solution.py:457

commit v3 on v2

--- a/solution.py
+++ b/solution.py
@@ -16,7 +16,7 @@
 C2 = 0.07216878364870323 * 1.4426950408889634
 EMPTY = -1e30
 TICK_R, TICK_D = 3, 6
-RELAYED = 6
+RELAYED = 4
 GROUPS = ((0, 4), (4, 8))
 CHIPS = sorted(
     [(dx, dy) for dy in range(4) for dx in range(4) if dx or dy],
@@ -167,14 +167,17 @@
     def merge_core(b):
         copy_c(b).wait_recv()
         merged = [merge_stats([pc[b, c, g, 8], cr[b, g, 8]]) for g in range(4)]
+        factors = [[[column(s, t) for s in shares] for t in range(4)] for shares, _ in merged]
         for g in range(4):
-            shares, stat = merged[g]
+            own, got = pc[b, c, g], cr[b, g]
+            sums = {8: merged[g][1]}
             for t in range(4):
-                f0, f1 = column(shares[0], t), column(shares[1], t)
+                f0, f1 = factors[g][t]
                 for i in range(4):
                     at = tile_at(t, i)
-                    mg[b, g, at] = f0 * pc[b, c, g, at] + f1 * cr[b, g, at]
-            mg[b, g, 8] = stat
+                    sums[at] = f0 * own[at] + f1 * got[at]
+            for at, tile in sums.items():
+                mg[b, g, at] = tile
 
     def copy_r(b, way):
         par = b % 2
@@ -190,16 +193,21 @@
     def relay(b):
         for way in range(2):
             copy_r(b, way).wait_recv()
+        sums = []
         for way in range(2):
             g = (position(b % 2) + 1 + 2 * way) % 4
-            mine = mg[b, g, 8]
-            shares, stat = merge_stats([mine, rr[b, way, 8 - 8 * way]])
+            own, got = mg[b, g, pl.ds(8 * way, 9)], rr[b, way]
+            stat_at = 8 - 8 * way
+            shares, stat = merge_stats([own[stat_at], got[stat_at]])
+            sums.append((g, 8, jnp.where((lane & 63) // 2 == way, stat, own[stat_at])))
             for t in (2 * way, 2 * way + 1):
                 f0, f1 = column(shares[0], t), column(shares[1], t)
                 for i in range(4):
                     at = tile_at(t, i)
-                    mg[b, g, at] = f0 * mg[b, g, at] + f1 * rr[b, way, at - 8 * way]
-            mg[b, g, 8] = jnp.where((lane & 63) // 2 == way, stat, mine)
+                    sums.append((g, at, f0 * own[at - 8 * way] + f1 * got[at - 8 * way]))
+        for g, at, tile in sums:
+            mg[b, g, at] = tile
+        for way in range(2):
             copy_p1(b, 1 + 2 * way).start()
 
     def send_p1(b):
@@ -212,11 +220,17 @@
             copy_p1(b, r).wait_recv()
         parts = [mg.at[b, position(b % 2)]] + [p1r.at[b, r - 1] for r in steps]
         shares, stat = merge_stats([part[8] for part in parts])
+        factors = [[column(s, t) for s in shares] for t in range(4)]
+        sums = []
         for t in range(4):
-            f = [column(s, t) for s in shares]
-            for i in range(4):
-                p2[b, t, i] = sum(f[n] * parts[n][tile_at(t, i)] for n in range(len(parts)))
-            p2[b, t, 4] = pltpu.roll(stat, 128 - t, 1) if t else stat
+            f = factors[t]
+            sums += [
+                (t, i, sum(f[n] * parts[n][tile_at(t, i)] for n in range(len(parts))))
+                for i in range(4)
+            ]
+            sums.append((t, 4, pltpu.roll(stat, 128 - t, 1) if t else stat))
+        for t, i, tile in sums:
+            p2[b, t, i] = tile
         for r in (2, 1, 3):
             copy_p2(b, r).start()
 
@@ -229,17 +243,23 @@
         top = functools.reduce(jnp.maximum, peaks)
         f = [jnp.exp2(p - top) for p in peaks]
         inverse = 1.0 / sum(a * b for a, b in zip(f, totals))
-        for i in range(4):
-            tile = sum(f[n] * parts[n][i] for n in range(4)) * inverse
-            att[b, :, i * 128 : i * 128 + 128] = head_major(tile)
+        tiles = [head_major(sum(f[n] * parts[n][i] for n in range(4)) * inverse) for i in range(4)]
+        for i, tile in enumerate(tiles):
+            att[b, :, i * 128 : i * 128 + 128] = tile
 
     def before(i):
         merge_core(i - 1)
-        start_relay(i - 1)
+        if isinstance(i, int):
+            (start_relay if i - 1 < RELAYED else send_p1)(i - 1)
+        elif RELAYED >= B - 3:
+            start_relay(i - 1)
+        else:
+            pl.when(i - 1 < RELAYED)(lambda: start_relay(i - 1))
+            pl.when(i - 1 >= RELAYED)(lambda: send_p1(i - 1))
 
     def services(i):
         if isinstance(i, int):
-            if i >= TICK_R:
+            if TICK_R <= i < TICK_R + RELAYED:
                 relay(i - TICK_R)
             if i >= TICK_D:
                 merge_first(i - TICK_D, True)
@@ -272,13 +292,8 @@
     services(B - 2)
     attend(B - 1, 1, False)
     copy_c(B - 1).start()
-    merge_core(B - 2)
-    send_p1(B - 2)
+    before(B - 1)
     services(B - 1)
-
-    def late_relay(b, _):
-        relay(b)
-        return 0
 
     def late_relayed(b, _):
         merge_first(b, True)
@@ -297,10 +312,12 @@
 
     merge_core(B - 1)
     send_p1(B - 1)
-    lax.fori_loop(B - TICK_R, RELAYED, late_relay, 0)
+    for b in range(B - TICK_R, RELAYED):
+        relay(b)
     lax.fori_loop(B - TICK_D, 4, late_relayed, 0)
     second(0, 2)
-    lax.fori_loop(4, RELAYED, late_relayed, 0)
+    if RELAYED > 4:
+        lax.fori_loop(4, RELAYED, late_relayed, 0)
     lax.fori_loop(RELAYED, B, late_direct, 0)
 
     sub = iota((8, 128), 0)
@@ -366,15 +383,17 @@
 
     load_vu.wait()
     load_w.wait()
-    second(2, GROUPS[0][1])
-    project(0)
-    second(GROUPS[0][1], B - 2)
+    at = 2
+    for n, (_, hi) in enumerate(GROUPS[:-1]):
+        second(at, hi)
+        project(n)
+        at = hi
+    second(at, B - 2)
     spread(0)
-    second(B - 2, B)
-    project(1)
-    spread(1)
-    finish(0)
-    finish(1)
+    second(max(at, B - 2), B)
+    project(len(GROUPS) - 1)
+    for n in range(1, len(GROUPS)):
+        spread(n)
 
     def drain(b, _):
         copy_c(b).wait_send()
@@ -399,6 +418,8 @@
         copy_y(n).wait_send()
         for to in range(15):
             copy_z(n, to).wait_send()
+    for n in range(len(GROUPS)):
+        finish(n)
 
 
 def local(queries, latent_cache, context_lengths, value_up, output_projection_rows):

time: 41.9 us -> 41.4 us (0.988)
  Pallas kernels: 41.2 us -> 40.7 us
    pallas_call x1, Pallas kernels: 41.2 us -> 40.7 us  [local(): pl.pallas_call(kernel, out_shape=pltpu.VMEM((B, NQ, DEV_COLS), f32), in_s...]
where the time goes in v3:
time: 41.4 us; the launch traced here: 41.3 us
  Pallas kernels  40.7 us (98%)
  other arithmetic  0.61 us (1%)
    pallas_call x1, Pallas kernels, local(): pl.pallas_call(kernel, out_shape=pltpu.VMEM((B, NQ, DEV_COLS), f32), in_s...  40.7 us

profile of v3, /device:TPU:1, one launch (start us, length us, event | category | flops | bytes accessed | tf_op | source)
XLA Modules:
  0.0 41.3 jit_solution(11848709527820021747)
XLA Ops:
  0.0 40.7 %attend_and_project.1 = f32[8,4,224]{2,1,0:T(4,128)S(1)} custom-call(bf16[8,256,576]{2,1,0:T(8,128)(2,1)} %bitcast.3, bf16[8,576,1024]{2,1,0:T(8,128)(2,1)} %bitcast.2, s32[8]{0:T(128)} %ctx_ref.1, bf16[2,512,128]{2,1,0:T(8,128)(2,1)} %vu_hbm.1, bf16[256,7168]{1,0:T(8,128)(2,1)} %w_hbm.1), custom_call_target="tpu_custom_call" | custom-call | tf_op jit(solution)/shard_map/attend_and_project/pallas_call | solution.py:428
  40.7 0.6 %convert_element_type.3 = bf16[8,4,224]{2,1,0:T(4,128)(2,1)} convert(f32[8,4,224]{2,1,0:T(4,128)S(1)} %attend_and_project.1) | non-fusion elementwise | flops 7168 | bytes 43008 | tf_op jit(solution)/shard_map/convert_element_type | solution.py:478

commit v4 on v3

--- a/solution.py
+++ b/solution.py
@@ -17,7 +17,7 @@
 EMPTY = -1e30
 TICK_R, TICK_D = 3, 6
 RELAYED = 4
-GROUPS = ((0, 4), (4, 8))
+GROUPS = ((0, 6), (6, 8))
 CHIPS = sorted(
     [(dx, dy) for dy in range(4) for dx in range(4) if dx or dy],
     key=lambda o: -(min(o[0], 4 - o[0]) + min(o[1], 4 - o[1])),

time: 41.4 us -> 43.3 us (1.046)
  Pallas kernels: 40.7 us -> 42.6 us
    pallas_call x1, Pallas kernels: 40.7 us -> 42.6 us  [local(): pl.pallas_call(kernel, out_shape=pltpu.VMEM((B, NQ, DEV_COLS), f32), in_s...]
where the time goes in v4:
time: 43.3 us
  Pallas kernels  42.6 us (98%)
  other arithmetic  0.61 us (1%)
    pallas_call x1, Pallas kernels, local(): pl.pallas_call(kernel, out_shape=pltpu.VMEM((B, NQ, DEV_COLS), f32), in_s...  42.6 us

profile of v4, /device:TPU:1, one launch (start us, length us, event | category | flops | bytes accessed | tf_op | source)
XLA Modules:
  0.0 43.3 jit_solution(8397009593651262071)
XLA Ops:
  0.0 42.6 %attend_and_project.1 = f32[8,4,224]{2,1,0:T(4,128)S(1)} custom-call(bf16[8,256,576]{2,1,0:T(8,128)(2,1)} %bitcast.3, bf16[8,576,1024]{2,1,0:T(8,128)(2,1)} %bitcast.2, s32[8]{0:T(128)} %ctx_ref.1, bf16[2,512,128]{2,1,0:T(8,128)(2,1)} %vu_hbm.1, bf16[256,7168]{1,0:T(8,128)(2,1)} %w_hbm.1), custom_call_target="tpu_custom_call" | custom-call | tf_op jit(solution)/shard_map/attend_and_project/pallas_call | solution.py:428
  42.6 0.6 %convert_element_type.3 = bf16[8,4,224]{2,1,0:T(4,128)(2,1)} convert(f32[8,4,224]{2,1,0:T(4,128)S(1)} %attend_and_project.1) | non-fusion elementwise | flops 7168 | bytes 43008 | tf_op jit(solution)/shard_map/convert_element_type | solution.py:478
